TPU v7x, 128 devices: a whole 4x4x4 slice. The times are simulated.
128 devices in a mesh: ctx: 32 (over z_hi, x, y), grp: 4 (over z_lo, core).
Axes of the slice: x: 4, y: 4, z: 4 (z_hi: 2, z_lo: 2; z = z_hi * 2 + z_lo), core: 2. Of those that a mesh axis runs over, the one named last changes fastest.
Arguments:
- prefill_queries: bfloat16 [4096, 40960], P('ctx', 'grp'), may hold values from -30 to 30
- latents: bfloat16 [4096, 1024], P('ctx', 'grp'), may hold values from -5 to 5
- rope_keys: bfloat16 [4096, 64], P('ctx'), may hold values from -5 to 5
- span_slots: int32 [64], replicated, may hold values from 0 to 63, each once
- decode_queries: bfloat16 [2, 256, 40960], P(None, 'ctx', 'grp'), may hold values from -30 to 30
- new_latents: bfloat16 [2, 256, 1024], P(None, 'ctx', 'grp'), may hold values from -5 to 5
- new_rope: bfloat16 [2, 256, 64], P(None, 'ctx'), may hold values from -5 to 5
- context_lengths: int32 [256], P('ctx'), may hold values from 1 to 1024, 131072 in all
- page_table: int32 [256, 16], P('ctx'), may hold values from 0 to 63
- value_up: bfloat16 [128, 256, 128], P('grp'), may hold values from -0.375 to 0.375
- out_proj: bfloat16 [16384, 7168], P('grp', 'ctx'), may hold values from -0.046875 to 0.046875
Outputs:
- prefill_values: bfloat16 [4096, 16384], P('ctx', 'grp')
- decoded: bfloat16 [2, 256, 7168], P(None, 'grp', 'ctx')
Inputs may be any that keep to these rules, and one draw needn't show every extreme that they name: `span_slots`: each of 0 to 63 stands once.
All inputs are finite; a program needn't handle non-finite values. No bound on the sum of `context_lengths` on one device may be relied on, other than what follows from the above.
Results may differ from a plain program's by a relative error of at most 0.015.
Values may be sent and summed in bfloat16 or wider, within the bound.
No kernel may reach another device: no remote copies, remote signals or barrier semaphores. Data moves between devices by JAX's collectives and lax.ppermute only.
A program may use at most 128 MiB of HBM per device.

v0:
```python
import math

import jax
import jax.numpy as jnp
from jax import lax
from jax.sharding import PartitionSpec as P

PAGE = 64


attention_score_scale = 192.0 ** (-0.5)
far_below = -1e30


def span_of_rows(row_ids, span_slots, span_len):
    slot_ids = jnp.arange(span_slots.shape[0], dtype=jnp.int32)
    matches = (row_ids // span_len)[:, None] == slot_ids[None, :]
    span_ids = jnp.sum(jnp.where(matches, span_slots[None, :], 0), axis=1)
    return span_ids * span_len + row_ids % span_len


def attend_block(carried, queries, query_pos, latent_rows, rope_rows, key_pos):
    run_max, run_sum, run_acc = carried
    latent_width = latent_rows.shape[1]
    scores = jnp.einsum(
        "qhd,kd->qhk", queries[:, :, :latent_width], latent_rows, preferred_element_type=jnp.float32
    )
    scores = scores + jnp.einsum(
        "qhd,kd->qhk", queries[:, :, latent_width:], rope_rows, preferred_element_type=jnp.float32
    )
    scores = scores * attention_score_scale
    visible = (query_pos[:, None] >= key_pos[None, :])[:, None, :]
    new_max = jnp.maximum(run_max, jnp.max(jnp.where(visible, scores, -jnp.inf), axis=2))
    rescale = jnp.exp(run_max - new_max)
    weights = jnp.where(visible, jnp.exp(scores - new_max[:, :, None]), 0.0)
    run_sum = run_sum * rescale + jnp.sum(weights, axis=2)
    run_acc = run_acc * rescale[:, :, None] + jnp.einsum(
        "qhk,kc->qhc", weights.astype(jnp.bfloat16), latent_rows, preferred_element_type=jnp.float32
    )
    return (new_max, run_sum, run_acc)


def fold_keys(carried, queries, query_pos, pieces, span_slots, span_len):
    latent_rows, rope_rows = pieces
    row_count = latent_rows.shape[0]
    block_rows = math.gcd(row_count, 512)
    block_count = row_count // block_rows
    key_pos = span_of_rows(jnp.arange(row_count, dtype=jnp.int32), span_slots, span_len)
    stacked = (
        latent_rows.reshape(block_count, block_rows, latent_rows.shape[1]),
        rope_rows.reshape(block_count, block_rows, rope_rows.shape[1]),
        key_pos.reshape(block_count, block_rows),
    )

    def one_step(state_in, block_item):
        latent_block, rotary_block_keys, pos_block = block_item
        state_out = attend_block(
            state_in, queries, query_pos, latent_block, rotary_block_keys, pos_block
        )
        return (state_out, None)

    return lax.scan(one_step, carried, stacked)[0]


def body(
    prefill_queries,
    latents,
    rope_keys,
    span_slots,
    decode_queries,
    new_latents,
    new_rope,
    context_lengths,
    page_table,
    value_up,
    out_proj,
):
    heads_local = value_up.shape[0]
    latent_width = latents.shape[1]
    rope_width = rope_keys.shape[1]
    key_width = latent_width + rope_width
    tok_local = latents.shape[0]
    span_len = tok_local // 2
    queries = prefill_queries.reshape(tok_local, heads_local, key_width)
    own_rows = lax.axis_index("ctx") * tok_local + jnp.arange(tok_local, dtype=jnp.int32)
    query_pos = span_of_rows(own_rows, span_slots, span_len)
    start_state = (
        jnp.full((tok_local, heads_local), far_below, jnp.float32),
        jnp.zeros((tok_local, heads_local), jnp.float32),
        jnp.zeros((tok_local, heads_local, latent_width), jnp.float32),
    )
    run_max, run_sum, run_acc = fold_keys(
        start_state,
        queries,
        query_pos,
        (
            lax.all_gather(latents, "ctx", axis=0, tiled=True),
            lax.all_gather(rope_keys, "ctx", axis=0, tiled=True),
        ),
        span_slots,
        span_len,
    )
    pooled_latent, pooled_rope = (
        lax.all_gather(latents, "ctx", axis=0, tiled=True),
        lax.all_gather(rope_keys, "ctx", axis=0, tiled=True),
    )
    attended = (run_acc / run_sum[:, :, None]).astype(jnp.bfloat16)
    prefill_values = jnp.einsum(
        "qhc,hcv->qhv", attended, value_up, preferred_element_type=jnp.float32
    ).astype(jnp.bfloat16)
    prefill_values = prefill_values.reshape(tok_local, heads_local * value_up.shape[2])
    steps_count = decode_queries.shape[0]
    rows_local = decode_queries.shape[1]
    max_len = page_table.shape[1] * PAGE
    slot_ids = jnp.arange(span_slots.shape[0], dtype=jnp.int32)
    inverse = jnp.sum(
        jnp.where(span_slots[:, None] == slot_ids[None, :], slot_ids[:, None], 0), axis=0
    )
    offsets = jnp.arange(max_len, dtype=jnp.int32)
    page_ids = jnp.repeat(page_table, PAGE, axis=1)
    token_pos = page_ids * PAGE + offsets[None, :] % PAGE
    span_ids = token_pos // span_len
    slot_of = jnp.sum(
        jnp.where(span_ids[:, :, None] == slot_ids[None, None, :], inverse[None, None, :], 0),
        axis=2,
    )
    storage = slot_of * span_len + token_pos % span_len
    cache_latent = pooled_latent[storage]
    cache_rope = pooled_rope[storage]
    step_queries = decode_queries.reshape(steps_count, rows_local, heads_local, key_width)
    cached_score_matrix = jnp.einsum(
        "wizx,iqx->wizq",
        step_queries[..., :latent_width],
        cache_latent,
        preferred_element_type=jnp.float32,
    )
    cached_score_matrix = (
        cached_score_matrix
        + jnp.einsum(
            "wizx,iqx->wizq",
            step_queries[..., latent_width:],
            cache_rope,
            preferred_element_type=jnp.float32,
        )
    ) * attention_score_scale
    fresh_scores = jnp.einsum(
        "sbhd,nbd->sbhn",
        step_queries[..., :latent_width],
        new_latents,
        preferred_element_type=jnp.float32,
    )
    fresh_scores = (
        fresh_scores
        + jnp.einsum(
            "sbhd,nbd->sbhn",
            step_queries[..., latent_width:],
            new_rope,
            preferred_element_type=jnp.float32,
        )
    ) * attention_score_scale
    visible_cache = (offsets[None, :] < context_lengths[:, None])[None, :, None, :]
    step_ids = jnp.arange(steps_count, dtype=jnp.int32)
    visible_fresh = (step_ids[None, :] <= step_ids[:, None])[:, None, None, :]
    row_max = jnp.maximum(
        jnp.max(jnp.where(visible_cache, cached_score_matrix, -jnp.inf), axis=3),
        jnp.max(jnp.where(visible_fresh, fresh_scores, -jnp.inf), axis=3),
    )
    cached_weight_matrix = jnp.where(
        visible_cache, jnp.exp(cached_score_matrix - row_max[..., None]), 0.0
    )
    fresh_weights = jnp.where(visible_fresh, jnp.exp(fresh_scores - row_max[..., None]), 0.0)
    totals = jnp.sum(cached_weight_matrix, axis=3) + jnp.sum(fresh_weights, axis=3)
    decode_attended = jnp.einsum(
        "sbhk,bkc->sbhc",
        cached_weight_matrix.astype(jnp.bfloat16),
        cache_latent,
        preferred_element_type=jnp.float32,
    )
    decode_attended = decode_attended + jnp.einsum(
        "sbhn,nbc->sbhc",
        fresh_weights.astype(jnp.bfloat16),
        new_latents,
        preferred_element_type=jnp.float32,
    )
    decode_attended = (decode_attended / totals[..., None]).astype(jnp.bfloat16)
    decode_values = jnp.einsum(
        "sbhc,hcv->sbhv", decode_attended, value_up, preferred_element_type=jnp.float32
    ).astype(jnp.bfloat16)
    decode_values = decode_values.reshape(steps_count, rows_local, heads_local * value_up.shape[2])
    partial_products = jnp.einsum(
        "sbk,kd->sbd",
        lax.all_gather(decode_values, "ctx", axis=1, tiled=True),
        out_proj,
        preferred_element_type=jnp.float32,
    )
    summed = lax.psum(partial_products.astype(jnp.bfloat16), "grp").astype(jnp.float32)
    row_share = partial_products.shape[1] // lax.axis_size("grp")
    decoded = lax.dynamic_slice_in_dim(summed, lax.axis_index("grp") * row_share, row_share, 1)
    return (prefill_values, decoded.astype(jnp.bfloat16))


def solution(mesh):
    placed = (
        P("ctx", "grp"),
        P("ctx", "grp"),
        P("ctx", None),
        P(),
        P(None, "ctx", "grp"),
        P(None, "ctx", "grp"),
        P(None, "ctx", None),
        P("ctx"),
        P("ctx", None),
        P("grp", None, None),
        P("grp", "ctx"),
    )
    return jax.shard_map(
        body,
        mesh=mesh,
        in_specs=placed,
        out_specs=(P("ctx", "grp"), P(None, "grp", "ctx")),
        check_vma=False,
    )
```

profile of v0, /device:TPU:34, one launch (start us, length us, event | category | flops | bytes accessed | tf_op | source)
XLA Modules:
  0.0 487.4 jit_solution(216696433196240585)
XLA Ops:
  13.6 90.7 %all_gather.12 = bf16[4096,64]{1,0:T(8,128)(2,1)S(1)} all-gather(bf16[128,64]{1,0:T(8,128)(2,1)} %copy.54), channel_id=1, replica_groups=mesh['ctx'=32,'grp'=4] {'ctx'}, dimensions={0}, use_global_device_ids=true | all-gather | bytes 540672 | tf_op jit(solution)/shard_map/all_gather | solution.py:98
  104.3 31.9 %gather_fusion.1 = bf16[8192,64]{1,0:T(8,128)(2,1)} fusion(bf16[4096,64]{1,0:T(8,128)(2,1)S(1)} %all_gather.12, s32[8192]{0:T(1024)} %bitcast_clamp_fusion), kind=kCustom, calls=%fused_computation.1 | custom fusion | bytes 2129920 | tf_op jit(solution)/shard_map/gather | solution.py:129
  151.2 32.8 %gather_fusion = bf16[8192,256]{1,0:T(8,128)(2,1)} fusion(bf16[4096,256]{1,0:T(8,128)(2,1)} %all-gather.3.cloned.1.call-done, s32[8192]{0:T(1024)S(1)} %copy-done.4), kind=kCustom, calls=%fused_computation | custom fusion | bytes 8421376 | tf_op jit(solution)/shard_map/gather | solution.py:128
  191.9 241.6 %while.15 = (s32[]{:T(128)}, f32[128,32]{0,1:T(8,128)S(1)}, f32[128,32]{0,1:T(8,128)S(1)}, f32[128,32,256]{2,0,1:T(8,128)}, s32[128]{0:T(128)S(1)}, /*index=5*/s...) while((s32[]{:T(128)}, f32[128,32]{0,1:T(8,128)S(1)}, ...), condition=%wide.region_5.6_spmd.clone, body=%wide.region_2.5_spmd.clone.sunk | while | flops 2440122368 | bytes 92872856 | solution.py:62
  191.9 6.2 %fusion.106 = f32[512,128,32]{1,0,2:T(8,128)} fusion(bf16[128,32,320]{2,0,1:T(8,128)(2,1)} %get-tuple-element.244, bf16[8,512,256]{2,1,0:T(8,128)(2,1)} %get-tuple-element.243, s32[]{:T(128)} %get-tuple-element.226), kind=kOutput, calls=%fused_computation.16.clone.1 | convolution fusion | flops 1073741824 | bytes 10748416 | tf_op jit(solution)/shard_map/while/body/eval_jaxpr/qhd,kd->qhk/dot_general | solution.py:25
  202.8 8.3 %fusion.107 = (f32[128,32]{0,1:T(8,128)S(1)}, f32[512,128,32]{1,0,2:T(8,128)}) fusion(pred[128,512]{0,1:T(8,128)(4,1)S(1)} %broadcast_compare_fusion.2, f32[512,128,32]{1,0,2:T(8,128)} %fusion.106, bf16[128,32,320]{0,2,1:T(8,128)(2,1)} %copy.113, bf16[8,512,64]{1,2,0:T(8,128)(2,1)} %get-tuple-element.245, s32[]{:T(128)} %get-tuple-element.226), kind=kOutput, calls=%fused_computation.4.clone.1 | convolution fusion | flops 276819968 | bytes 17449472 | tf_op jit(solution)/shard_map/while/body/eval_jaxpr/qhd,kd->qhk/dot_general | solution.py:28
  221.5 6.2 %fusion.106 = f32[512,128,32]{1,0,2:T(8,128)} fusion(bf16[128,32,320]{2,0,1:T(8,128)(2,1)} %get-tuple-element.244, bf16[8,512,256]{2,1,0:T(8,128)(2,1)} %get-tuple-element.243, s32[]{:T(128)} %get-tuple-element.226), kind=kOutput, calls=%fused_computation.16.clone.1 | convolution fusion | flops 1073741824 | bytes 10748416 | tf_op jit(solution)/shard_map/while/body/eval_jaxpr/qhd,kd->qhk/dot_general | solution.py:25
  232.5 8.3 %fusion.107 = (f32[128,32]{0,1:T(8,128)S(1)}, f32[512,128,32]{1,0,2:T(8,128)}) fusion(pred[128,512]{0,1:T(8,128)(4,1)S(1)} %broadcast_compare_fusion.2, f32[512,128,32]{1,0,2:T(8,128)} %fusion.106, bf16[128,32,320]{0,2,1:T(8,128)(2,1)} %copy.113, bf16[8,512,64]{1,2,0:T(8,128)(2,1)} %get-tuple-element.245, s32[]{:T(128)} %get-tuple-element.226), kind=kOutput, calls=%fused_computation.4.clone.1 | convolution fusion | flops 276819968 | bytes 17449472 | tf_op jit(solution)/shard_map/while/body/eval_jaxpr/qhd,kd->qhk/dot_general | solution.py:28
  246.7 5.3 %fusion.110 = f32[128,32,256]{2,0,1:T(8,128)} fusion(f32[128,32,256]{2,0,1:T(8,128)} %get-tuple-element.229, f32[128,32]{0,1:T(8,128)S(1)} %get-tuple-element.214, pred[]{:T(512)S(6)} %compare.31, f32[512,128,32]{1,0,2:T(8,128)S(1)} %copy-done.1, f32[128,32]{0,1:T(8,128)S(1)} %select_maximum_fusion.2, ...), kind=kOutput, calls=%fused_computation.12.clone.1 | convolution fusion | flops 1083179008 | bytes 17138176 | tf_op jit(solution)/shard_map/while/body/eval_jaxpr/qhk,kc->qhc/dot_general | solution.py:37
  252.0 6.2 %fusion.106 = f32[512,128,32]{1,0,2:T(8,128)} fusion(bf16[128,32,320]{2,0,1:T(8,128)(2,1)} %get-tuple-element.244, bf16[8,512,256]{2,1,0:T(8,128)(2,1)} %get-tuple-element.243, s32[]{:T(128)} %get-tuple-element.226), kind=kOutput, calls=%fused_computation.16.clone.1 | convolution fusion | flops 1073741824 | bytes 10748416 | tf_op jit(solution)/shard_map/while/body/eval_jaxpr/qhd,kd->qhk/dot_general | solution.py:25
  262.9 8.3 %fusion.107 = (f32[128,32]{0,1:T(8,128)S(1)}, f32[512,128,32]{1,0,2:T(8,128)}) fusion(pred[128,512]{0,1:T(8,128)(4,1)S(1)} %broadcast_compare_fusion.2, f32[512,128,32]{1,0,2:T(8,128)} %fusion.106, bf16[128,32,320]{0,2,1:T(8,128)(2,1)} %copy.113, bf16[8,512,64]{1,2,0:T(8,128)(2,1)} %get-tuple-element.245, s32[]{:T(128)} %get-tuple-element.226), kind=kOutput, calls=%fused_computation.4.clone.1 | convolution fusion | flops 276819968 | bytes 17449472 | tf_op jit(solution)/shard_map/while/body/eval_jaxpr/qhd,kd->qhk/dot_general | solution.py:28
  277.0 5.3 %fusion.110 = f32[128,32,256]{2,0,1:T(8,128)} fusion(f32[128,32,256]{2,0,1:T(8,128)} %get-tuple-element.229, f32[128,32]{0,1:T(8,128)S(1)} %get-tuple-element.214, pred[]{:T(512)S(6)} %compare.31, f32[512,128,32]{1,0,2:T(8,128)S(1)} %copy-done.1, f32[128,32]{0,1:T(8,128)S(1)} %select_maximum_fusion.2, ...), kind=kOutput, calls=%fused_computation.12.clone.1 | convolution fusion | flops 1083179008 | bytes 17138176 | tf_op jit(solution)/shard_map/while/body/eval_jaxpr/qhk,kc->qhc/dot_general | solution.py:37
  282.3 6.2 %fusion.106 = f32[512,128,32]{1,0,2:T(8,128)} fusion(bf16[128,32,320]{2,0,1:T(8,128)(2,1)} %get-tuple-element.244, bf16[8,512,256]{2,1,0:T(8,128)(2,1)} %get-tuple-element.243, s32[]{:T(128)} %get-tuple-element.226), kind=kOutput, calls=%fused_computation.16.clone.1 | convolution fusion | flops 1073741824 | bytes 10748416 | tf_op jit(solution)/shard_map/while/body/eval_jaxpr/qhd,kd->qhk/dot_general | solution.py:25
  293.2 8.3 %fusion.107 = (f32[128,32]{0,1:T(8,128)S(1)}, f32[512,128,32]{1,0,2:T(8,128)}) fusion(pred[128,512]{0,1:T(8,128)(4,1)S(1)} %broadcast_compare_fusion.2, f32[512,128,32]{1,0,2:T(8,128)} %fusion.106, bf16[128,32,320]{0,2,1:T(8,128)(2,1)} %copy.113, bf16[8,512,64]{1,2,0:T(8,128)(2,1)} %get-tuple-element.245, s32[]{:T(128)} %get-tuple-element.226), kind=kOutput, calls=%fused_computation.4.clone.1 | convolution fusion | flops 276819968 | bytes 17449472 | tf_op jit(solution)/shard_map/while/body/eval_jaxpr/qhd,kd->qhk/dot_general | solution.py:28
  307.2 5.3 %fusion.110 = f32[128,32,256]{2,0,1:T(8,128)} fusion(f32[128,32,256]{2,0,1:T(8,128)} %get-tuple-element.229, f32[128,32]{0,1:T(8,128)S(1)} %get-tuple-element.214, pred[]{:T(512)S(6)} %compare.31, f32[512,128,32]{1,0,2:T(8,128)S(1)} %copy-done.1, f32[128,32]{0,1:T(8,128)S(1)} %select_maximum_fusion.2, ...), kind=kOutput, calls=%fused_computation.12.clone.1 | convolution fusion | flops 1083179008 | bytes 17138176 | tf_op jit(solution)/shard_map/while/body/eval_jaxpr/qhk,kc->qhc/dot_general | solution.py:37
  312.5 6.2 %fusion.106 = f32[512,128,32]{1,0,2:T(8,128)} fusion(bf16[128,32,320]{2,0,1:T(8,128)(2,1)} %get-tuple-element.244, bf16[8,512,256]{2,1,0:T(8,128)(2,1)} %get-tuple-element.243, s32[]{:T(128)} %get-tuple-element.226), kind=kOutput, calls=%fused_computation.16.clone.1 | convolution fusion | flops 1073741824 | bytes 10748416 | tf_op jit(solution)/shard_map/while/body/eval_jaxpr/qhd,kd->qhk/dot_general | solution.py:25
  323.4 8.3 %fusion.107 = (f32[128,32]{0,1:T(8,128)S(1)}, f32[512,128,32]{1,0,2:T(8,128)}) fusion(pred[128,512]{0,1:T(8,128)(4,1)S(1)} %broadcast_compare_fusion.2, f32[512,128,32]{1,0,2:T(8,128)} %fusion.106, bf16[128,32,320]{0,2,1:T(8,128)(2,1)} %copy.113, bf16[8,512,64]{1,2,0:T(8,128)(2,1)} %get-tuple-element.245, s32[]{:T(128)} %get-tuple-element.226), kind=kOutput, calls=%fused_computation.4.clone.1 | convolution fusion | flops 276819968 | bytes 17449472 | tf_op jit(solution)/shard_map/while/body/eval_jaxpr/qhd,kd->qhk/dot_general | solution.py:28
  342.7 6.2 %fusion.106 = f32[512,128,32]{1,0,2:T(8,128)} fusion(bf16[128,32,320]{2,0,1:T(8,128)(2,1)} %get-tuple-element.244, bf16[8,512,256]{2,1,0:T(8,128)(2,1)} %get-tuple-element.243, s32[]{:T(128)} %get-tuple-element.226), kind=kOutput, calls=%fused_computation.16.clone.1 | convolution fusion | flops 1073741824 | bytes 10748416 | tf_op jit(solution)/shard_map/while/body/eval_jaxpr/qhd,kd->qhk/dot_general | solution.py:25
  353.6 8.3 %fusion.107 = (f32[128,32]{0,1:T(8,128)S(1)}, f32[512,128,32]{1,0,2:T(8,128)}) fusion(pred[128,512]{0,1:T(8,128)(4,1)S(1)} %broadcast_compare_fusion.2, f32[512,128,32]{1,0,2:T(8,128)} %fusion.106, bf16[128,32,320]{0,2,1:T(8,128)(2,1)} %copy.113, bf16[8,512,64]{1,2,0:T(8,128)(2,1)} %get-tuple-element.245, s32[]{:T(128)} %get-tuple-element.226), kind=kOutput, calls=%fused_computation.4.clone.1 | convolution fusion | flops 276819968 | bytes 17449472 | tf_op jit(solution)/shard_map/while/body/eval_jaxpr/qhd,kd->qhk/dot_general | solution.py:28
  373.0 6.2 %fusion.106 = f32[512,128,32]{1,0,2:T(8,128)} fusion(bf16[128,32,320]{2,0,1:T(8,128)(2,1)} %get-tuple-element.244, bf16[8,512,256]{2,1,0:T(8,128)(2,1)} %get-tuple-element.243, s32[]{:T(128)} %get-tuple-element.226), kind=kOutput, calls=%fused_computation.16.clone.1 | convolution fusion | flops 1073741824 | bytes 10748416 | tf_op jit(solution)/shard_map/while/body/eval_jaxpr/qhd,kd->qhk/dot_general | solution.py:25
  383.9 8.3 %fusion.107 = (f32[128,32]{0,1:T(8,128)S(1)}, f32[512,128,32]{1,0,2:T(8,128)}) fusion(pred[128,512]{0,1:T(8,128)(4,1)S(1)} %broadcast_compare_fusion.2, f32[512,128,32]{1,0,2:T(8,128)} %fusion.106, bf16[128,32,320]{0,2,1:T(8,128)(2,1)} %copy.113, bf16[8,512,64]{1,2,0:T(8,128)(2,1)} %get-tuple-element.245, s32[]{:T(128)} %get-tuple-element.226), kind=kOutput, calls=%fused_computation.4.clone.1 | convolution fusion | flops 276819968 | bytes 17449472 | tf_op jit(solution)/shard_map/while/body/eval_jaxpr/qhd,kd->qhk/dot_general | solution.py:28
  403.2 6.2 %fusion.106 = f32[512,128,32]{1,0,2:T(8,128)} fusion(bf16[128,32,320]{2,0,1:T(8,128)(2,1)} %get-tuple-element.244, bf16[8,512,256]{2,1,0:T(8,128)(2,1)} %get-tuple-element.243, s32[]{:T(128)} %get-tuple-element.226), kind=kOutput, calls=%fused_computation.16.clone.1 | convolution fusion | flops 1073741824 | bytes 10748416 | tf_op jit(solution)/shard_map/while/body/eval_jaxpr/qhd,kd->qhk/dot_general | solution.py:25
  414.1 8.3 %fusion.107 = (f32[128,32]{0,1:T(8,128)S(1)}, f32[512,128,32]{1,0,2:T(8,128)}) fusion(pred[128,512]{0,1:T(8,128)(4,1)S(1)} %broadcast_compare_fusion.2, f32[512,128,32]{1,0,2:T(8,128)} %fusion.106, bf16[128,32,320]{0,2,1:T(8,128)(2,1)} %copy.113, bf16[8,512,64]{1,2,0:T(8,128)(2,1)} %get-tuple-element.245, s32[]{:T(128)} %get-tuple-element.226), kind=kOutput, calls=%fused_computation.4.clone.1 | convolution fusion | flops 276819968 | bytes 17449472 | tf_op jit(solution)/shard_map/while/body/eval_jaxpr/qhd,kd->qhk/dot_general | solution.py:28
  443.0 36.4 %all-reduce.2.cloned.1.call-done = bf16[2,256,224]{2,1,0:T(8,128)(2,1)} async-done(((bf16[2,256,224]{2,1,0:T(8,128)(2,1)}), bf16[2,256,224]{2,1,0:T(8,128)(2,1)}) %all-reduce.2.cloned.1.call-update) | async-done | bytes 229392 | tf_op jit(solution)/shard_map/psum | solution.py:196
  (145 shorter events, 149.9 us)
Async XLA Ops:
  7.2 183.3 %copy-start = (bf16[32,256,128]{2,1,0:T(8,128)(2,1)S(1)}, bf16[32,256,128]{2,1,0:T(8,128)(2,1)}, u32[]{:S(2)}) copy-start(bf16[32,256,128]{2,1,0:T(8,128)(2,1)} %param.22) | copy-start | bytes 6291460
  7.2 144.0 %all-gather.3.cloned.1.call-start = ((), (), s32[]{:S(2)}) async-start(), calls=%async_computation | async-start | bytes 2162688 | tf_op jit(solution)/shard_map/all_gather | solution.py:97
  7.9 425.5 %all-gather.5.cloned.1.call-start = ((), (), s32[]{:S(2)}) async-start(), calls=%async_computation.1 | async-start | bytes 4325376 | tf_op jit(solution)/shard_map/all_gather | solution.py:192
  141.7 4.6 copy-start.5
  141.7 5.0 %copy-start.6 = (s32[8]{0:T(128)S(1)}, s32[8]{0:T(128)}, u32[]{:S(2)}) copy-start(s32[8]{0:T(128)} %param.20) | copy-start | bytes 100
  141.7 5.1 %copy-start.7 = (bf16[2,8,256]{2,1,0:T(8,128)(2,1)S(1)}, bf16[2,8,256]{2,1,0:T(8,128)(2,1)}, u32[]{:S(2)}) copy-start(bf16[2,8,256]{2,1,0:T(8,128)(2,1)} %param.18) | copy-start | bytes 24580
  141.7 5.4 %copy-start.8 = (bf16[2,8,64]{2,1,0:T(8,128)(2,1)S(1)}, bf16[2,8,64]{2,1,0:T(8,128)(2,1)}, u32[]{:S(2)}) copy-start(bf16[2,8,64]{2,1,0:T(8,128)(2,1)} %param.19) | copy-start | bytes 6148
  146.3 4.9 %copy-start.4 = (s32[8192]{0:T(1024)S(1)}, s32[8192]{0:T(1024)}, u32[]{:S(2)}) copy-start(s32[8192]{0:T(1024)} %bitcast_clamp_fusion) | copy-start | bytes 98308
  184.0 5.1 %copy-start.2 = (bf16[8192,256]{1,0:T(8,128)(2,1)S(1)}, bf16[8192,256]{1,0:T(8,128)(2,1)}, u32[]{:S(2)}) copy-start(bf16[8192,256]{1,0:T(8,128)(2,1)} %gather_fusion) | copy-start | bytes 12582916
  190.0 1.9 copy-start.3
  191.7 287.8 %all-reduce.2.cloned.1.call-start = ((), (), s32[]{:S(2)}) async-start(), calls=%async_computation.2 | async-start | bytes 524288 | tf_op jit(solution)/shard_map/psum | solution.py:196
  211.1 5.8 %copy-start.1 = (f32[512,128,32]{1,0,2:T(8,128)S(1)}, f32[512,128,32]{1,0,2:T(8,128)}, u32[]{:S(2)}) copy-start(f32[512,128,32]{1,0,2:T(8,128)} %get-tuple-element.212) | copy-start | bytes 25165828 | tf_op jit(solution)/shard_map/while
  240.9 5.8 %copy-start.1 = (f32[512,128,32]{1,0,2:T(8,128)S(1)}, f32[512,128,32]{1,0,2:T(8,128)}, u32[]{:S(2)}) copy-start(f32[512,128,32]{1,0,2:T(8,128)} %get-tuple-element.212) | copy-start | bytes 25165828 | tf_op jit(solution)/shard_map/while
  271.1 5.8 %copy-start.1 = (f32[512,128,32]{1,0,2:T(8,128)S(1)}, f32[512,128,32]{1,0,2:T(8,128)}, u32[]{:S(2)}) copy-start(f32[512,128,32]{1,0,2:T(8,128)} %get-tuple-element.212) | copy-start | bytes 25165828 | tf_op jit(solution)/shard_map/while
  301.4 5.8 %copy-start.1 = (f32[512,128,32]{1,0,2:T(8,128)S(1)}, f32[512,128,32]{1,0,2:T(8,128)}, u32[]{:S(2)}) copy-start(f32[512,128,32]{1,0,2:T(8,128)} %get-tuple-element.212) | copy-start | bytes 25165828 | tf_op jit(solution)/shard_map/while
  331.7 5.8 %copy-start.1 = (f32[512,128,32]{1,0,2:T(8,128)S(1)}, f32[512,128,32]{1,0,2:T(8,128)}, u32[]{:S(2)}) copy-start(f32[512,128,32]{1,0,2:T(8,128)} %get-tuple-element.212) | copy-start | bytes 25165828 | tf_op jit(solution)/shard_map/while
  361.9 5.8 %copy-start.1 = (f32[512,128,32]{1,0,2:T(8,128)S(1)}, f32[512,128,32]{1,0,2:T(8,128)}, u32[]{:S(2)}) copy-start(f32[512,128,32]{1,0,2:T(8,128)} %get-tuple-element.212) | copy-start | bytes 25165828 | tf_op jit(solution)/shard_map/while
  392.2 5.8 %copy-start.1 = (f32[512,128,32]{1,0,2:T(8,128)S(1)}, f32[512,128,32]{1,0,2:T(8,128)}, u32[]{:S(2)}) copy-start(f32[512,128,32]{1,0,2:T(8,128)} %get-tuple-element.212) | copy-start | bytes 25165828 | tf_op jit(solution)/shard_map/while
  422.4 5.8 %copy-start.1 = (f32[512,128,32]{1,0,2:T(8,128)S(1)}, f32[512,128,32]{1,0,2:T(8,128)}, u32[]{:S(2)}) copy-start(f32[512,128,32]{1,0,2:T(8,128)} %get-tuple-element.212) | copy-start | bytes 25165828 | tf_op jit(solution)/shard_map/while
Sparse Core Ops, SparseCore 0:
  11.1 72.3 all-gather.2
  191.8 86.3 all-gather.4
  438.4 41.0 all-reduce.1
where the time goes:
time: 492 us; the launch traced here: 487 us
  matrix products  176 us (36%)
  local copies, waits for them, and re-layouts  122 us (25%)
  blocking collectives  90.7 us (18%)
  other arithmetic  46.6 us (9%)
  waiting for transfers between devices  37.1 us (8%)
  between operations  14 us (3%)
    all_gather x1, blocking collectives, body(): lax.all_gather(rope_keys, 'ctx', axis=0, tiled=True)  90.7 us
    dot_general x8, matrix products, attend_block(): jnp.einsum('qhd,kd->qhk', queries[:, :, latent_width:], rope_rows, prefer...  66.2 us
    dot_general x8, matrix products, attend_block(): jnp.einsum('qhd,kd->qhk', queries[:, :, :latent_width], latent_rows, pref...  49.6 us
    while x32, local copies, waits for them, and re-layouts  42.4 us
    dot_general x8, matrix products, attend_block(): jnp.einsum('qhk,kc->qhc', weights.astype(jnp.bfloat16), latent_rows, pref...  41.7 us
    reduce_sum x8, other arithmetic, attend_block(): run_sum = run_sum * rescale + jnp.sum(weights, axis=2)  40.1 us
    psum x1, waiting for transfers between devices, body(): lax.psum(partial_products.astype(jnp.bfloat16), 'grp').astype(jnp.float32)  36.4 us
    gather x1, local copies, waits for them, and re-layouts, body(): cache_latent = pooled_latent[storage]  32.8 us
  transfers between devices with their start and end apart: 3, of which 1 were waited for; matrix products, arithmetic and copies ran while one was open for 60% of the time, Pallas kernels for 0%

commit v1 on v0

v1 whole, which is shorter than its diff:
```python
import functools
import itertools
import math

import jax
import jax.numpy as jnp
from jax import lax
from jax.experimental import pallas as pl
from jax.experimental.pallas import tpu as pltpu
from jax.sharding import PartitionSpec as P

SPAN = 64
LATENT = 256
ROPE = 64
KEYW = LATENT + ROPE
KPAD = 384
VDIM = 128

HEADS_TILE = 8
ROWS = HEADS_TILE * SPAN
KEYS = 512

EXP2_SCALE = 192.0 ** -0.5 * math.log2(math.e)
FAR_BELOW = -1e30
NT = (((1,), (1,)), ((), ()))
Z, X, Y = 2, 4, 4


def ctx_index(z, x, y):
    return z * (X * Y) + x * Y + y


def places():
    return [(z, x, y) for z in range(Z) for x in range(X) for y in range(Y)]


def from_other_z(value):
    pairs = [(ctx_index(z, x, y), ctx_index(1 - z, x, y)) for z, x, y in places()]
    return lax.ppermute(value, "ctx", pairs)


def gather(block, axes):
    lines = {}
    for z, x, y in places():
        at = (z, None if "x" in axes else x, None if "y" in axes else y)
        lines.setdefault(at, []).append(ctx_index(z, x, y))
    groups = list(lines.values())
    copies = jnp.broadcast_to(block[None], (len(groups[0]),) + block.shape)
    return lax.all_to_all(
        copies, "ctx", split_axis=0, concat_axis=0, axis_index_groups=groups, tiled=True
    )


def pack_kernel(latents_ref, rope_ref, out_ref):
    rope = rope_ref[...].astype(jnp.float32).T
    for span in range(2):
        rows = slice(span * SPAN, (span + 1) * SPAN)
        out_ref[span, :SPAN, :] = latents_ref[rows, :]
        parts = [rope[span * SPAN + c * 16 : span * SPAN + (c + 1) * 16] for c in range(4)]
        out_ref[span, SPAN:, :] = jnp.concatenate(parts, axis=1).astype(jnp.bfloat16)


def pack(latents, rope_keys):
    return pl.pallas_call(
        pack_kernel,
        out_shape=jax.ShapeDtypeStruct((2, SPAN + SPAN // 4, LATENT), jnp.bfloat16),
    )(latents, rope_keys.T)


def decode_kernel(
    z_ref,
    spans_ref,
    pages_ref,
    lengths_ref,
    own_first_ref,
    other_first_ref,
    second_ref,
    q_ref,
    new_latents_ref,
    new_rope_ref,
    up_hbm,
    keys_hbm,
    values_ref,
    up_ref,
    keys_ref,
    queries,
    fresh,
    cache,
    att,
    sems,
):
    low_lanes = lax.broadcasted_iota(jnp.int32, (16, 128), 1) < ROPE
    up_copy = pltpu.make_async_copy(up_hbm, up_ref, sems.at[0])
    up_copy.start()
    for half, dz, line in itertools.product(range(2), range(2), range(X * Y)):
        block = own_first_ref.at[line] if half == 0 else second_ref.at[line, dz]
        if half == 0 and dz == 1:
            block = other_first_ref.at[line]
        z = z_ref[0] if dz == 0 else 1 - z_ref[0]
        span = spans_ref[2 * (z * (X * Y) + line) + half]
        rows = pl.ds(pl.multiple_of(span * SPAN, SPAN), SPAN)
        keys_ref[rows, :LATENT] = block[:SPAN, :]
        packed = block[SPAN:, :].astype(jnp.float32)
        parts = []
        for c in range(2):
            two = packed[:, c * 128 : (c + 1) * 128]
            parts.append(jnp.where(low_lanes, two, 0.0))
            parts.append(jnp.where(low_lanes, pltpu.roll(two, 64, 1), 0.0))
        keys_ref[rows, LATENT:] = jnp.concatenate(parts, axis=0).astype(jnp.bfloat16)
    keys_copy = pltpu.make_async_copy(keys_ref, keys_hbm, sems.at[1])
    keys_copy.start()

    rows_local, pages = pages_ref.shape
    slots = pages * SPAN
    width = cache.shape[1]
    fresh[...] = jnp.zeros_like(fresh)
    for s in range(2):
        for h in range(32):
            at = h // 2 * 2 * KEYW + h % 2 * 256
            rows = q_ref[s, :, at : at + KPAD].astype(jnp.float32)
            if h % 2:
                rows = pltpu.roll(rows, KPAD - 64, 1)
            for c in range(3):
                queries[c, pl.ds(s * 32 + h, rows_local, stride=64), :] = rows[
                    :, c * 128 : (c + 1) * 128
                ]
        mine = pl.ds(s, rows_local, stride=16)
        latent_rows = new_latents_ref[s].astype(jnp.float32)
        fresh[0, mine, :] = latent_rows[:, :128]
        fresh[1, mine, :] = latent_rows[:, 128:]
        rope_rows = new_rope_ref[s].astype(jnp.float32)
        fresh[2, mine, :] = jnp.concatenate([rope_rows, jnp.zeros_like(rope_rows)], axis=1)

    def whole(ref, rows):
        return jnp.concatenate([ref[c, rows, :] for c in range(3)], axis=1).astype(jnp.bfloat16)

    cols = lax.broadcasted_iota(jnp.int32, (64, width), 1)
    step = lax.broadcasted_iota(jnp.int32, (64, width), 0) // 32
    fresh_seen = (cols >= slots) & (cols - slots <= step)
    for b in range(rows_local):
        for j in range(pages):
            page = pages_ref[b, j]
            cache[b, j * SPAN : (j + 1) * SPAN, :] = keys_ref[
                pl.ds(pl.multiple_of(page * SPAN, SPAN), SPAN), :
            ]
        cache[b, slots : slots + 16, :] = whole(fresh, slice(b * 16, (b + 1) * 16))
        cache[b, slots + 16 :, :] = jnp.zeros((width - slots - 16, KPAD), jnp.bfloat16)
        row_queries = whole(queries, slice(b * 64, (b + 1) * 64))
        scores = lax.dot_general(row_queries, cache[b], NT, preferred_element_type=jnp.float32)
        seen = (cols < lengths_ref[b]) | fresh_seen
        scores = jnp.where(seen, scores, FAR_BELOW)
        top = jnp.max(scores, axis=1, keepdims=True)
        weights = jnp.exp2(scores * EXP2_SCALE - top * EXP2_SCALE)
        total = jnp.sum(weights, axis=1, keepdims=True)
        attended = jnp.dot(
            weights.astype(jnp.bfloat16), cache[b, :, :LATENT], preferred_element_type=jnp.float32
        )
        attended = attended / total
        for s in range(2):
            for c in range(2):
                att[c, pl.ds(s * rows_local + b, 32, stride=16), :] = attended[
                    s * 32 : (s + 1) * 32, c * 128 : (c + 1) * 128
                ]
    up_copy.wait()
    for h in range(32):
        mine = slice(h * 16, (h + 1) * 16)
        attended = jnp.concatenate([att[0, mine, :], att[1, mine, :]], axis=1)
        values_ref[:, h * VDIM : (h + 1) * VDIM] = jnp.dot(
            attended.astype(jnp.bfloat16), up_ref[h], preferred_element_type=jnp.float32
        ).astype(jnp.bfloat16)
    keys_copy.wait()


def decode(
    z, spans, pages, lengths, own_first, other_first, second, queries, latents, rope, value_up
):
    smem = pl.BlockSpec(memory_space=pltpu.SMEM)
    vmem = pl.BlockSpec(memory_space=pltpu.VMEM)
    hbm = pl.BlockSpec(memory_space=pl.ANY)
    rows_local = pages.shape[0]
    heads = value_up.shape[0]
    return pl.pallas_call(
        decode_kernel,
        out_shape=(
            jax.ShapeDtypeStruct((spans.shape[0] * SPAN, KPAD), jnp.bfloat16),
            jax.ShapeDtypeStruct((2 * rows_local, heads * VDIM), jnp.bfloat16),
        ),
        in_specs=[smem] * 4 + [vmem] * 6 + [hbm],
        out_specs=(hbm, vmem),
        scratch_shapes=[
            pltpu.VMEM(value_up.shape, jnp.bfloat16),
            pltpu.VMEM((spans.shape[0] * SPAN, KPAD), jnp.bfloat16),
            pltpu.VMEM((3, 64 * rows_local, 128), jnp.float32),
            pltpu.VMEM((3, 16 * rows_local, 128), jnp.float32),
            pltpu.VMEM((rows_local, pages.shape[1] * SPAN + 128, KPAD), jnp.bfloat16),
            pltpu.VMEM((2, 16 * heads, 128), jnp.float32),
            pltpu.SemaphoreType.DMA((2,)),
        ],
        compiler_params=pltpu.CompilerParams(vmem_limit_bytes=40 << 20),
        cost_estimate=pl.CostEstimate(
            flops=2 * 8 * 64 * 1152 * 640, bytes_accessed=12 << 20, transcendentals=8 * 64 * 1152
        ),
    )(
        z, spans, pages, lengths, own_first, other_first, second, queries, latents, rope, value_up
    )


def prefill_kernel(spans_ref, q_hbm, k_hbm, up_hbm, out_ref, done_ref, *scratch):
    q_ref, k_ref, up_ref, qs, s_a, s_b, p_a, p_b, top, total, r_a, r_b, acc, sems = scratch
    q_copy = pltpu.make_async_copy(q_hbm, q_ref, sems.at[0])
    k_copy = pltpu.make_async_copy(k_hbm, k_ref, sems.at[1])
    up_copy = pltpu.make_async_copy(up_hbm, up_ref, sems.at[2])
    q_copy.start()
    k_copy.start()
    up_copy.start()
    top[...] = jnp.full(top.shape, FAR_BELOW, jnp.float32)
    total[...] = jnp.zeros_like(total)
    acc[...] = jnp.zeros_like(acc)
    p_b[...] = jnp.zeros_like(p_b)
    r_b[...] = jnp.ones_like(r_b)
    q_copy.wait()
    tiles = acc.shape[0] // 2
    span_of = [spans_ref[s] for s in range(2)]
    blocks_of = [span // (KEYS // SPAN) for span in span_of]

    for tile in range(tiles):
        for pair in range(HEADS_TILE // 2):
            at = (tile * HEADS_TILE + pair * 2) * KEYW
            for s in range(2):
                tokens = slice(s * SPAN, (s + 1) * SPAN)
                rows = qs.at[2 * tile + s]
                rows[2 * pair * SPAN : (2 * pair + 1) * SPAN, :] = q_ref[tokens, at : at + KPAD]
                odd = q_ref[tokens, at + 256 : at + 640].astype(jnp.float32)
                rows[(2 * pair + 1) * SPAN : (2 * pair + 2) * SPAN, :] = pltpu.roll(
                    odd, KPAD - 64, 1
                ).astype(jnp.bfloat16)

    def key_rows(block):
        return pl.ds(pl.multiple_of(block * KEYS, KEYS), KEYS)

    def score(unit, block, s_ref):
        s_ref[...] = lax.dot_general(
            qs[unit], k_ref[key_rows(block), :], NT, preferred_element_type=jnp.float32
        )

    lead = lax.broadcasted_iota(jnp.int32, (SPAN, 128), 1)
    lead = lead - lax.broadcasted_iota(jnp.int32, (SPAN, 128), 0)

    def weigh(unit, s_ref, p_ref, r_ref, last_key=None):
        for h in range(HEADS_TILE):
            rows = slice(h * SPAN, (h + 1) * SPAN)
            parts = [s_ref[rows, c * 128 : (c + 1) * 128] for c in range(KEYS // 128)]
            if last_key is not None:
                parts = [
                    jnp.where(lead <= last_key - c * 128, part, FAR_BELOW)
                    for c, part in enumerate(parts)
                ]
            highest = functools.reduce(jnp.maximum, parts)
            old = top[unit, rows]
            new = jnp.maximum(old, jnp.max(highest, axis=1, keepdims=True))
            top[unit, rows] = new
            scaled = new * EXP2_SCALE
            rescale = jnp.exp2(old * EXP2_SCALE - scaled)
            r_ref[rows] = rescale
            weights = [jnp.exp2(part * EXP2_SCALE - scaled) for part in parts]
            total[unit, rows] = total[unit, rows] * rescale + sum(weights)
            for c, weight in enumerate(weights):
                p_ref[rows, c * 128 : (c + 1) * 128] = weight.astype(jnp.bfloat16)

    def add_values(unit, block, p_ref, r_ref):
        product = jnp.dot(
            p_ref[...], k_ref[key_rows(block), :LATENT], preferred_element_type=jnp.float32
        )
        r = r_ref[...]
        acc[unit, :, :128] = acc[unit, :, :128] * r + product[:, :128]
        acc[unit, :, 128:] = acc[unit, :, 128:] * r + product[:, 128:]

    k_copy.wait()

    def last_item(unit):
        return unit, jnp.where(unit % 2 == 0, blocks_of[0], blocks_of[1])

    def following(item):
        unit, block = item
        ends = block + 1 >= jnp.where(unit % 2 == 0, blocks_of[0], blocks_of[1])
        other = 1 - unit % 2
        other_empty = jnp.where(other == 0, blocks_of[0], blocks_of[1]) == 0
        jump = jnp.where(other_empty, 2, 1)
        unit = jnp.where(ends, unit + jump, unit)
        return unit, jnp.where(ends, 0, block + 1)

    def two_items(i, carry):
        before, here = carry[:2], carry[2:]
        after = following(here)
        score(*after, s_b)
        weigh(here[0], s_a, p_a, r_a)
        add_values(*before, p_b, r_b)
        later = following(after)
        at_end = later[0] >= 2 * tiles
        later = tuple(jnp.where(at_end, end, value) for end, value in zip(last_item(0), later))
        score(*later, s_a)
        weigh(after[0], s_b, p_b, r_b)
        add_values(*here, p_a, r_a)
        return after + later

    all_blocks = blocks_of[0] + blocks_of[1]
    first = (jnp.where(blocks_of[0] == 0, 1, 0), jnp.int32(0))
    first = tuple(
        jnp.where(all_blocks == 0, end, value) for end, value in zip(last_item(0), first)
    )
    score(*first, s_a)
    carry = lax.fori_loop(
        0, all_blocks * (tiles // 2), two_items, (jnp.int32(0), jnp.int32(0)) + first
    )

    def two_last(i, carry):
        before = carry
        even, odd = last_item(2 * i), last_item(2 * i + 1)
        later = last_item(jnp.minimum(2 * i + 2, 2 * tiles - 1))
        offset = [(span_of[s] - blocks_of[s] * (KEYS // SPAN)) * SPAN for s in range(2)]
        score(*odd, s_b)
        weigh(even[0], s_a, p_a, r_a, offset[0])
        add_values(*before, p_b, r_b)
        score(*later, s_a)
        weigh(odd[0], s_b, p_b, r_b, offset[1])
        add_values(*even, p_a, r_a)
        return odd

    before = lax.fori_loop(0, tiles, two_last, carry[:2])
    add_values(*before, p_b, r_b)

    up_copy.wait()

    def finish(tile, carry):
        for s in range(2):
            unit = 2 * tile + s
            attended = acc[unit] / jnp.sum(total[unit], axis=1, keepdims=True)
            attended = attended.astype(jnp.bfloat16)
            values = [
                jnp.dot(
                    attended[h * SPAN : (h + 1) * SPAN],
                    up_ref[tile * HEADS_TILE + h],
                    preferred_element_type=jnp.float32,
                ).astype(jnp.bfloat16)
                for h in range(HEADS_TILE)
            ]
            columns = HEADS_TILE * VDIM
            out_ref[
                s * SPAN : (s + 1) * SPAN, pl.ds(pl.multiple_of(tile * columns, columns), columns)
            ] = jnp.concatenate(values, axis=1)
        return carry

    lax.fori_loop(0, tiles, finish, 0)
    done_ref[...] = jnp.zeros_like(done_ref)


def prefill(spans, queries, keys, value_up):
    tokens = queries.shape[0]
    heads = value_up.shape[0]
    units = 2 * heads // HEADS_TILE
    f32 = jnp.float32
    smem = pl.BlockSpec(memory_space=pltpu.SMEM)
    vmem = pl.BlockSpec(memory_space=pltpu.VMEM)
    return pl.pallas_call(
        prefill_kernel,
        out_shape=(
            jax.ShapeDtypeStruct((tokens, heads * VDIM), jnp.bfloat16),
            jax.ShapeDtypeStruct((8, 128), f32),
        ),
        in_specs=[smem] + [pl.BlockSpec(memory_space=pl.ANY)] * 3,
        out_specs=(vmem, vmem),
        scratch_shapes=[
            pltpu.VMEM(queries.shape, jnp.bfloat16),
            pltpu.VMEM(keys.shape, jnp.bfloat16),
            pltpu.VMEM(value_up.shape, jnp.bfloat16),
            pltpu.VMEM((units, ROWS, KPAD), jnp.bfloat16),
            pltpu.VMEM((ROWS, KEYS), f32),
            pltpu.VMEM((ROWS, KEYS), f32),
            pltpu.VMEM((ROWS, KEYS), jnp.bfloat16),
            pltpu.VMEM((ROWS, KEYS), jnp.bfloat16),
            pltpu.VMEM((units, ROWS, 128), f32),
            pltpu.VMEM((units, ROWS, 128), f32),
            pltpu.VMEM((ROWS, 128), f32),
            pltpu.VMEM((ROWS, 128), f32),
            pltpu.VMEM((units, ROWS, LATENT), f32),
            pltpu.SemaphoreType.DMA((3,)),
        ],
        compiler_params=pltpu.CompilerParams(vmem_limit_bytes=48 << 20),
        cost_estimate=pl.CostEstimate(
            flops=units * ROWS * keys.shape[0] * 640,
            bytes_accessed=8 << 20,
            transcendentals=units * ROWS * keys.shape[0] // 2,
        ),
    )(spans, queries, keys, value_up)


def project_kernel(place_ref, rows_ref, w_ref, other_w_ref, after_ref, *refs):
    out_refs, sums = refs[:4], refs[4]
    z, head_z, head_core = place_ref[0], place_ref[1] // 2, place_ref[1] % 2
    for side, weights in enumerate((w_ref, other_w_ref)):
        sums[side] = lax.dot_general(
            rows_ref[...], weights[...], NT, preferred_element_type=jnp.float32
        )
    share = sums.shape[1] // 2
    for k, out_ref in enumerate(out_refs):
        to_z, to_core = (head_z + k // 2) % 2, (head_core + k) % 2
        side = jnp.where(to_z == z, 0, 1)
        rows = pl.ds(pl.multiple_of(to_core * share, share), share)
        out_ref[...] = sums[side, rows, :].astype(jnp.bfloat16)


def project(place, rows, weights, other_weights, after):
    smem = pl.BlockSpec(memory_space=pltpu.SMEM)
    vmem = pl.BlockSpec(memory_space=pltpu.VMEM)
    width, depth = weights.shape
    row_count = rows.shape[0]
    return pl.pallas_call(
        project_kernel,
        out_shape=(jax.ShapeDtypeStruct((row_count // 2, width), jnp.bfloat16),) * 4,
        in_specs=[smem, vmem, vmem, vmem, pl.BlockSpec(memory_space=pl.ANY)],
        out_specs=(vmem,) * 4,
        scratch_shapes=[pltpu.VMEM((2, row_count, width), jnp.float32)],
        compiler_params=pltpu.CompilerParams(vmem_limit_bytes=24 << 20),
        cost_estimate=pl.CostEstimate(
            flops=4 * row_count * depth * 256, bytes_accessed=8 << 20, transcendentals=0
        ),
    )(place, rows, weights, other_weights, after)


def share_out(k, part):
    pairs = [
        (ctx_index(z, x, y) * 4 + 2 * a + b, ctx_index(a ^ k // 2, x, y) * 4 + 2 * z + (b ^ k % 2))
        for z, x, y in places()
        for a in range(2)
        for b in range(2)
    ]
    return lax.ppermute(part, ("ctx", "grp"), pairs)


def body(
    prefill_queries,
    latents,
    rope_keys,
    span_slots,
    decode_queries,
    new_latents,
    new_rope,
    context_lengths,
    page_table,
    value_up,
    out_proj,
):
    ctx = lax.axis_index("ctx").astype(jnp.int32)
    grp = lax.axis_index("grp").astype(jnp.int32)
    rows_local = page_table.shape[0]
    own_spans = lax.dynamic_slice_in_dim(span_slots, 2 * ctx, 2)

    z = ctx // (X * Y)
    own = pack(latents, rope_keys)
    second = jnp.stack([own[1], from_other_z(own[1])])
    own_first = gather(own[0], "xy")
    other_first = from_other_z(own_first)
    second = gather(second, "xy").reshape(X * Y, 2, *own.shape[1:])
    weights = out_proj.T
    other_weights = from_other_z(weights)
    keys, decode_values = decode(
        z.reshape(1),
        span_slots,
        page_table,
        context_lengths,
        own_first.reshape(X * Y, *own.shape[1:]),
        other_first.reshape(X * Y, *own.shape[1:]),
        second,
        decode_queries,
        new_latents,
        new_rope,
        value_up,
    )
    all_values = gather(decode_values, "xy").reshape(-1, decode_values.shape[1])
    prefill_values, prefill_done = prefill(own_spans, prefill_queries, keys, value_up)
    place = jnp.stack([z, grp])
    parts = project(place, all_values, weights, other_weights, prefill_done)
    summed = sum(share_out(k, part).astype(jnp.float32) for k, part in enumerate(parts))
    decoded = summed.astype(jnp.bfloat16).reshape(-1, 2, rows_local, summed.shape[1])
    decoded = decoded.transpose(1, 0, 2, 3).reshape(2, -1, summed.shape[1])
    return (prefill_values, decoded)


def solution(mesh):
    placed = (
        P("ctx", "grp"),
        P("ctx", "grp"),
        P("ctx", None),
        P(),
        P(None, "ctx", "grp"),
        P(None, "ctx", "grp"),
        P(None, "ctx", None),
        P("ctx"),
        P("ctx", None),
        P("grp", None, None),
        P("grp", "ctx"),
    )
    return jax.shard_map(
        body,
        mesh=mesh,
        in_specs=placed,
        out_specs=(P("ctx", "grp"), P(None, "grp", "ctx")),
        check_vma=False,
    )
```

time: 492 us -> 131 us (0.27); the launches traced: 487 us -> 133 us
  matrix products: 176 us -> 0 us
  local copies, waits for them, and re-layouts: 122 us -> 13.3 us
  blocking collectives: 90.7 us -> 0 us
  Pallas kernels: 0 us -> 58.7 us
  other arithmetic: 46.6 us -> 0.12 us
  starting transfers between devices: 0.3 us -> 34.2 us
  between operations: 14 us -> 0.79 us
  waiting for transfers between devices: 37.1 us -> 25.8 us
    dot_general x33 -> x0, matrix products: 176 us -> none  [the longest x8 66.2 us: attend_block(): jnp.einsum('qhd,kd->qhk', queries[:, :, latent_width:], rope_rows, prefer...]
    all_gather x1 -> x0, blocking collectives: 90.7 us -> none  [body(): lax.all_gather(rope_keys, 'ctx', axis=0, tiled=True)]
    gather x2 -> x0, local copies, waits for them, and re-layouts: 64.6 us -> none  [the longest x1 32.8 us: body(): cache_latent = pooled_latent[storage]]
    pallas_call x0 -> x4, Pallas kernels: none -> 58.7 us  [the longest x1 46.9 us: prefill(): pl.pallas_call(prefill_kernel, out_shape=(jax.ShapeDtypeStruct((tokens, h...]
    while x32 -> x0, local copies, waits for them, and re-layouts: 42.4 us -> none
    reduce_sum x14 -> x0, other arithmetic: 42.3 us -> none  [the longest x8 40.1 us: attend_block(): run_sum = run_sum * rescale + jnp.sum(weights, axis=2)]
    psum x1 -> x0, waiting for transfers between devices: 36.4 us -> none  [body(): lax.psum(partial_products.astype(jnp.bfloat16), 'grp').astype(jnp.float32)]
    ppermute x0 -> x7, waiting for transfers between devices: none -> 19.9 us  [the longest x3 15.7 us: from_other_z(): return lax.ppermute(value, 'ctx', pairs)]
  transfers between devices with their start and end apart: 3 -> 10, of which waited for: 1 -> 7; matrix products, arithmetic and copies ran while one was open for 60% -> 0% of each run, Pallas kernels for 0% -> 35%
where the time goes in v1:
time: 131 us; the launch traced here: 133 us
  Pallas kernels  58.7 us (45%)
  starting transfers between devices  34.2 us (26%)
  waiting for transfers between devices  25.8 us (20%)
  local copies, waits for them, and re-layouts  13.3 us (10%)
    pallas_call x1, Pallas kernels, prefill(): pl.pallas_call(prefill_kernel, out_shape=(jax.ShapeDtypeStruct((tokens, h...  46.9 us
    all_to_all x3, starting transfers between devices, gather(): lax.all_to_all(copies, 'ctx', split_axis=0, concat_axis=0, axis_index_gro...  19.8 us
    ppermute x3, waiting for transfers between devices, from_other_z(): return lax.ppermute(value, 'ctx', pairs)  15.7 us
    ppermute x3, starting transfers between devices, from_other_z(): return lax.ppermute(value, 'ctx', pairs)  8.93 us
    unnamed x22, local copies, waits for them, and re-layouts  8.06 us
    pallas_call x1, Pallas kernels, decode(): pl.pallas_call(decode_kernel, out_shape=(jax.ShapeDtypeStruct((spans.shap...  7.29 us
    all_to_all x3, waiting for transfers between devices, gather(): lax.all_to_all(copies, 'ctx', split_axis=0, concat_axis=0, axis_index_gro...  5.91 us
    ppermute x4, starting transfers between devices, share_out(): return lax.ppermute(part, ('ctx', 'grp'), pairs)  5.5 us
  transfers between devices with their start and end apart: 10, of which 7 were waited for; matrix products, arithmetic and copies ran while one was open for 0% of the time, Pallas kernels for 35%

profile of v1, /device:TPU:34, one launch (start us, length us, event | category | flops | bytes accessed | tf_op | source)
XLA Modules:
  0.0 132.9 jit_solution(3276214218757868964)
XLA Ops:
  0.6 1.6 %shard_map.122 = bf16[2,80,256]{2,1,0:T(8,128)(2,1)} custom-call(bf16[128,256]{1,0:T(8,128)(2,1)} %latents_ref.1, bf16[64,128]{1,0:T(8,128)(2,1)} %bitcast.22), custom_call_target="tpu_custom_call" | custom-call | tf_op jit(solution)/shard_map/pallas_call | solution.py:64
  4.0 7.5 %all-to-all-start = ((bf16[16,80,256]{2,1,0:T(8,128)(2,1)}), bf16[16,80,256]{2,1,0:T(8,128)(2,1)S(1)}, u32[]{:S(2)}, u32[]{:S(2)}) async-start(bf16[16,80,256]{2,1,0:T(8,128)(2,1)} %broadcast_in_dim.9), calls=%async_computation | async-start | bytes 1310720 | tf_op jit(solution)/shard_map/all_to_all | solution.py:49
  11.4 3.0 %collective-permute-start.1 = (bf16[80,256]{1,0:T(8,128)(2,1)S(1)}, bf16[80,256]{1,0:T(8,128)(2,1)S(1)}, u32[]{:S(2)}, u32[]{:S(2)}) collective-permute-start(bf16[80,256]{1,0:T(8,128)(2,1)S(1)} %get-tuple-element.19), channel_id=1, source_target_pairs={{0,64},{4,68},{8,72},{12,76},{16,80},{20,84},{24,88},{28,92},{32,9... | collective-permute-start | bytes 122888 | tf_op jit(solution)/shard_map/ppermute | solution.py:39
  14.4 2.5 %collective-permute-done.1 = bf16[80,256]{1,0:T(8,128)(2,1)S(1)} collective-permute-done((bf16[80,256]{1,0:T(8,128)(2,1)S(1)}, bf16[80,256]{1,0:T(8,128)(2,1)S(1)}, u32[]{:S(2)}, u32[]{:S(2)}) %collective-permute-start.1) | collective-permute-done | bytes 40992 | tf_op jit(solution)/shard_map/ppermute | solution.py:39
  17.0 5.0 %all-to-all-done.own_first_ref = bf16[16,80,256]{2,1,0:T(8,128)(2,1)S(1)} async-done(((bf16[16,80,256]{2,1,0:T(8,128)(2,1)}), bf16[16,80,256]{2,1,0:T(8,128)(2,1)S(1)}, u32[]{:S(2)}, u32[]{:S(2)}) %all-to-all-start) | async-done | bytes 655392 | tf_op jit(solution)/shard_map/all_to_all | solution.py:49
  22.1 1.2 broadcast_in_dim.10
  23.2 5.9 %all-to-all-start.1 = ((bf16[16,2,80,256]{3,2,1,0:T(8,128)(2,1)}), bf16[16,2,80,256]{3,2,1,0:T(8,128)(2,1)S(1)}, u32[]{:S(2)}, u32[]{:S(2)}) async-start(bf16[16,2,80,256]{3,2,1,0:T(8,128)(2,1)} %broadcast_in_dim.10), calls=%async_computation.1 | async-start | bytes 2621440 | tf_op jit(solution)/shard_map/all_to_all | solution.py:49
  29.1 3.0 %collective-permute-start = (bf16[16,80,256]{2,1,0:T(8,128)(2,1)S(1)}, bf16[16,80,256]{2,1,0:T(8,128)(2,1)S(1)}, u32[]{:S(2)}, u32[]{:S(2)}) collective-permute-start(bf16[16,80,256]{2,1,0:T(8,128)(2,1)S(1)} %all-to-all-done.own_first_ref), channel_id=1, source_target_pairs={{0,64},{4,68},{8,72},{12,76},{16,80},{20,84},{24,88},{28,92},{32,9... | collective-permute-start | bytes 1966088 | tf_op jit(solution)/shard_map/ppermute | solution.py:39
  32.1 13.1 %collective-permute-done.other_first_ref = bf16[16,80,256]{2,1,0:T(8,128)(2,1)S(1)} collective-permute-done((bf16[16,80,256]{2,1,0:T(8,128)(2,1)S(1)}, bf16[16,80,256]{2,1,0:T(8,128)(2,1)S(1)}, u32[]{:S(2)}, u32[]{:S(2)}) %collective-permute-start) | collective-permute-done | bytes 655392 | tf_op jit(solution)/shard_map/ppermute | solution.py:39
  46.2 1.6 %copy-done = bf16[32,256,128]{2,1,0:T(8,128)(2,1)S(1)} copy-done((bf16[32,256,128]{2,1,0:T(8,128)(2,1)S(1)}, bf16[32,256,128]{2,1,0:T(8,128)(2,1)}, u32[]{:S(2)}) %copy-start) | copy-done | bytes 2097176
  47.8 7.3 %shard_map.123 = (bf16[4096,384]{1,0:T(8,128)(2,1)S(1)}, bf16[16,4096]{1,0:T(8,128)(2,1)S(1)}) custom-call(s32[1]{0:T(128)} %bitcast.z_ref, s32[64]{0:T(128)S(1)} %copy-done.8, s32[8,16]{1,0:T(8,128)S(1)} %copy-done.5, s32[8]{0:T(128)S(1)} %copy-done.7, bf16[16,80,256]{2,1,0:T(8,128)(2,1)S(1)} %all-to-all-done.own_first_ref, ...), custom_call_target="tpu_custom_call" | custom-call | flops 754974720 | bytes 12582912 | tf_op jit(solution)/shard_map/pallas_call | solution.py:182
  55.1 1.6 %copy-done.9 = bf16[4096,384]{1,0:T(8,128)(2,1)} copy-done((bf16[4096,384]{1,0:T(8,128)(2,1)}, bf16[4096,384]{1,0:T(8,128)(2,1)S(1)}, u32[]{:S(2)}) %copy-start.9) | copy-done | bytes 3145752
  56.7 1.6 %broadcast_in_dim.22 = bf16[16,16,4096]{2,1,0:T(8,128)(2,1)} broadcast(bf16[16,4096]{1,0:T(8,128)(2,1)S(1)} %get-tuple-element.12), dimensions={1,2} | broadcast | bytes 2228224 | tf_op jit(solution)/shard_map/broadcast_in_dim | solution.py:48
  58.3 6.4 %all-to-all-start.2 = ((bf16[16,16,4096]{2,1,0:T(8,128)(2,1)}), bf16[16,16,4096]{2,1,0:T(8,128)(2,1)S(1)}, u32[]{:S(2)}, u32[]{:S(2)}) async-start(bf16[16,16,4096]{2,1,0:T(8,128)(2,1)} %broadcast_in_dim.22), calls=%async_computation.2 | async-start | bytes 4194304 | tf_op jit(solution)/shard_map/all_to_all | solution.py:49
  64.7 3.0 %collective-permute-start.2 = (bf16[224,4096]{1,0:T(8,128)(2,1)}, bf16[224,4096]{1,0:T(8,128)(2,1)}, u32[]{:S(2)}, u32[]{:S(2)}) collective-permute-start(bf16[224,4096]{1,0:T(8,128)(2,1)} %bitcast.17), channel_id=1, source_target_pairs={{0,64},{4,68},{8,72},{12,76},{16,80},{20,84},{24,88},{28,92},{32,9... | collective-permute-start | bytes 5505032 | tf_op jit(solution)/shard_map/ppermute | solution.py:39
  67.8 1.6 %copy-done.1 = bf16[32,256,128]{2,1,0:T(8,128)(2,1)S(1)} copy-done((bf16[32,256,128]{2,1,0:T(8,128)(2,1)S(1)}, bf16[32,256,128]{2,1,0:T(8,128)(2,1)}, u32[]{:S(2)}) %copy-start.1) | copy-done | bytes 2097176
  69.4 1.7 %copy-done.10 = bf16[128,10240]{1,0:T(8,128)(2,1)S(1)} copy-done((bf16[128,10240]{1,0:T(8,128)(2,1)S(1)}, bf16[128,10240]{1,0:T(8,128)(2,1)}, u32[]{:S(2)}) %copy-start.10) | copy-done | bytes 2621464
  71.2 46.9 %shard_map.124 = (bf16[128,4096]{1,0:T(8,128)(2,1)}, f32[8,128]{1,0:T(8,128)S(1)}) custom-call(s32[2]{0:T(128)S(1)} %dynamic_slice.3.spans_ref, bf16[128,10240]{1,0:T(8,128)(2,1)S(1)} %copy-done.10, bf16[4096,384]{1,0:T(8,128)(2,1)} %copy-done.9, bf16[32,256,128]{2,1,0:T(8,128)(2,1)S(1)} %copy-done.1), custom_call_target="tpu_custom_call" | custom-call | flops 10737418240 | bytes 8388608 | tf_op jit(solution)/shard_map/pallas_call | solution.py:364
  118.1 1.5 %copy-done.2 = bf16[4096,224]{0,1:T(8,128)(2,1)S(1)} copy-done((bf16[4096,224]{0,1:T(8,128)(2,1)S(1)}, bf16[4096,224]{0,1:T(8,128)(2,1)}, u32[]{:S(2)}) %copy-start.2) | copy-done | bytes 1835032
  119.6 2.8 %shard_map.125 = (bf16[128,224]{1,0:T(8,128)(2,1)S(1)}, bf16[128,224]{1,0:T(8,128)(2,1)S(1)}, bf16[128,224]{1,0:T(8,128)(2,1)S(1)}, bf16[128,224]{1,0:T(8,128)(2,1)S(1)}) custom-call(s32[2]{0:T(128)S(1)} %pad_add_fusion.place_ref, bf16[256,4096]{1,0:T(8,128)(2,1)S(1)} %bitcast.16, bf16[224,4096]{1,0:T(8,128)(2,1)S(1)} %bitcast.18, ...), custom_call_target="tpu_custom_call" | custom-call | flops 1073741824 | bytes 8388608 | tf_op jit(solution)/shard_map/pallas_call | solution.py:417
  123.6 2.4 %collective-permute-start.4 = (bf16[128,224]{1,0:T(8,128)(2,1)S(1)}, bf16[128,224]{1,0:T(8,128)(2,1)S(1)}, u32[]{:S(2)}, u32[]{:S(2)}) collective-permute-start(bf16[128,224]{1,0:T(8,128)(2,1)S(1)} %get-tuple-element.15), channel_id=1, source_target_pairs={{0,1},{1,0},{2,65},{3,64},{4,5},{5,4},{6,69},{7,68},{8,9},{9,8},{1... | collective-permute-start | bytes 172040 | tf_op jit(solution)/shard_map/ppermute | solution.py:437
  126.0 1.9 %collective-permute-start.3 = (bf16[128,224]{1,0:T(8,128)(2,1)S(1)}, bf16[128,224]{1,0:T(8,128)(2,1)S(1)}, u32[]{:S(2)}, u32[]{:S(2)}) collective-permute-start(bf16[128,224]{1,0:T(8,128)(2,1)S(1)} %get-tuple-element.14), channel_id=1, source_target_pairs={{0,0},{1,1},{2,64},{3,65},{4,4},{5,5},{6,68},{7,69},{8,8},{9,9},{1... | collective-permute-start | bytes 172040 | tf_op jit(solution)/shard_map/ppermute | solution.py:437
  129.1 1.2 collective-permute-done.4
  130.3 1.9 %collective-permute-done.3 = bf16[128,224]{1,0:T(8,128)(2,1)S(1)} collective-permute-done((bf16[128,224]{1,0:T(8,128)(2,1)S(1)}, bf16[128,224]{1,0:T(8,128)(2,1)S(1)}, u32[]{:S(2)}, u32[]{:S(2)}) %collective-permute-start.3) | collective-permute-done | bytes 57376 | tf_op jit(solution)/shard_map/ppermute | solution.py:437
  (31 shorter events, 5.7 us)
Async XLA Ops:
  4.0 18.1 %all-to-all-start = ((bf16[16,80,256]{2,1,0:T(8,128)(2,1)}), bf16[16,80,256]{2,1,0:T(8,128)(2,1)S(1)}, u32[]{:S(2)}, u32[]{:S(2)}) async-start(bf16[16,80,256]{2,1,0:T(8,128)(2,1)} %broadcast_in_dim.9), calls=%async_computation | async-start | bytes 1310720 | tf_op jit(solution)/shard_map/all_to_all | solution.py:49
  11.4 5.5 %collective-permute-start.1 = (bf16[80,256]{1,0:T(8,128)(2,1)S(1)}, bf16[80,256]{1,0:T(8,128)(2,1)S(1)}, u32[]{:S(2)}, u32[]{:S(2)}) collective-permute-start(bf16[80,256]{1,0:T(8,128)(2,1)S(1)} %get-tuple-element.19), channel_id=1, source_target_pairs={{0,64},{4,68},{8,72},{12,76},{16,80},{20,84},{24,88},{28,92},{32,9... | collective-permute-start | bytes 122888 | tf_op jit(solution)/shard_map/ppermute | solution.py:39
  17.0 29.2 %copy-start.3 = (bf16[2,8,10240]{2,1,0:T(8,128)(2,1)S(1)}, bf16[2,8,10240]{2,1,0:T(8,128)(2,1)}, u32[]{:S(2)}) copy-start(bf16[2,8,10240]{2,1,0:T(8,128)(2,1)} %q_ref.1) | copy-start | bytes 983044
  17.0 29.2 %copy-start.4 = (bf16[2,8,256]{2,1,0:T(8,128)(2,1)S(1)}, bf16[2,8,256]{2,1,0:T(8,128)(2,1)}, u32[]{:S(2)}) copy-start(bf16[2,8,256]{2,1,0:T(8,128)(2,1)} %new_latents_ref.1) | copy-start | bytes 24580
  17.0 29.2 %copy-start.5 = (s32[8,16]{1,0:T(8,128)S(1)}, s32[8,16]{1,0:T(8,128)}, u32[]{:S(2)}) copy-start(s32[8,16]{1,0:T(8,128)} %pages_ref.1) | copy-start | bytes 1540
  17.0 29.2 %copy-start.6 = (bf16[2,8,64]{2,1,0:T(8,128)(2,1)S(1)}, bf16[2,8,64]{2,1,0:T(8,128)(2,1)}, u32[]{:S(2)}) copy-start(bf16[2,8,64]{2,1,0:T(8,128)(2,1)} %new_rope_ref.1) | copy-start | bytes 6148
  17.0 29.2 %copy-start.7 = (s32[8]{0:T(128)S(1)}, s32[8]{0:T(128)}, u32[]{:S(2)}) copy-start(s32[8]{0:T(128)} %lengths_ref.1) | copy-start | bytes 100
  17.0 29.2 %copy-start.8 = (s32[64]{0:T(128)S(1)}, s32[64]{0:T(128)}, u32[]{:S(2)}) copy-start(s32[64]{0:T(128)} %spans_ref.1) | copy-start | bytes 772
  23.2 22.9 %all-to-all-start.1 = ((bf16[16,2,80,256]{3,2,1,0:T(8,128)(2,1)}), bf16[16,2,80,256]{3,2,1,0:T(8,128)(2,1)S(1)}, u32[]{:S(2)}, u32[]{:S(2)}) async-start(bf16[16,2,80,256]{3,2,1,0:T(8,128)(2,1)} %broadcast_in_dim.10), calls=%async_computation.1 | async-start | bytes 2621440 | tf_op jit(solution)/shard_map/all_to_all | solution.py:49
  29.1 16.1 %collective-permute-start = (bf16[16,80,256]{2,1,0:T(8,128)(2,1)S(1)}, bf16[16,80,256]{2,1,0:T(8,128)(2,1)S(1)}, u32[]{:S(2)}, u32[]{:S(2)}) collective-permute-start(bf16[16,80,256]{2,1,0:T(8,128)(2,1)S(1)} %all-to-all-done.own_first_ref), channel_id=1, source_target_pairs={{0,64},{4,68},{8,72},{12,76},{16,80},{20,84},{24,88},{28,92},{32,9... | collective-permute-start | bytes 1966088 | tf_op jit(solution)/shard_map/ppermute | solution.py:39
  46.2 1.6 %copy-start = (bf16[32,256,128]{2,1,0:T(8,128)(2,1)S(1)}, bf16[32,256,128]{2,1,0:T(8,128)(2,1)}, u32[]{:S(2)}) copy-start(bf16[32,256,128]{2,1,0:T(8,128)(2,1)} %up_hbm.3) | copy-start | bytes 6291460
  55.1 1.6 %copy-start.9 = (bf16[4096,384]{1,0:T(8,128)(2,1)}, bf16[4096,384]{1,0:T(8,128)(2,1)S(1)}, u32[]{:S(2)}) copy-start(bf16[4096,384]{1,0:T(8,128)(2,1)S(1)} %get-tuple-element.10.k_hbm) | copy-start | bytes 9437188
  58.3 59.8 %all-to-all-start.2 = ((bf16[16,16,4096]{2,1,0:T(8,128)(2,1)}), bf16[16,16,4096]{2,1,0:T(8,128)(2,1)S(1)}, u32[]{:S(2)}, u32[]{:S(2)}) async-start(bf16[16,16,4096]{2,1,0:T(8,128)(2,1)} %broadcast_in_dim.22), calls=%async_computation.2 | async-start | bytes 4194304 | tf_op jit(solution)/shard_map/all_to_all | solution.py:49
  64.7 53.3 %collective-permute-start.2 = (bf16[224,4096]{1,0:T(8,128)(2,1)}, bf16[224,4096]{1,0:T(8,128)(2,1)}, u32[]{:S(2)}, u32[]{:S(2)}) collective-permute-start(bf16[224,4096]{1,0:T(8,128)(2,1)} %bitcast.17), channel_id=1, source_target_pairs={{0,64},{4,68},{8,72},{12,76},{16,80},{20,84},{24,88},{28,92},{32,9... | collective-permute-start | bytes 5505032 | tf_op jit(solution)/shard_map/ppermute | solution.py:39
  67.8 1.6 %copy-start.1 = (bf16[32,256,128]{2,1,0:T(8,128)(2,1)S(1)}, bf16[32,256,128]{2,1,0:T(8,128)(2,1)}, u32[]{:S(2)}) copy-start(bf16[32,256,128]{2,1,0:T(8,128)(2,1)} %up_hbm.3) | copy-start | bytes 6291460
  69.4 1.7 %copy-start.10 = (bf16[128,10240]{1,0:T(8,128)(2,1)S(1)}, bf16[128,10240]{1,0:T(8,128)(2,1)}, u32[]{:S(2)}) copy-start(bf16[128,10240]{1,0:T(8,128)(2,1)} %q_hbm.1) | copy-start | bytes 7864324
  118.1 1.5 %copy-start.2 = (bf16[4096,224]{0,1:T(8,128)(2,1)S(1)}, bf16[4096,224]{0,1:T(8,128)(2,1)}, u32[]{:S(2)}) copy-start(bf16[4096,224]{0,1:T(8,128)(2,1)} %param.21) | copy-start | bytes 5505028
  122.4 5.5 %collective-permute-start.6 = (bf16[128,224]{1,0:T(8,128)(2,1)S(1)}, bf16[128,224]{1,0:T(8,128)(2,1)S(1)}, u32[]{:S(2)}, u32[]{:S(2)}) collective-permute-start(bf16[128,224]{1,0:T(8,128)(2,1)S(1)} %get-tuple-element.17), channel_id=1, source_target_pairs={{0,65},{1,64},{2,1},{3,0},{4,69},{5,68},{6,5},{7,4},{8,73},{9,72},... | collective-permute-start | bytes 172040 | tf_op jit(solution)/shard_map/ppermute | solution.py:437
  122.5 6.6 %collective-permute-start.5 = (bf16[128,224]{1,0:T(8,128)(2,1)S(1)}, bf16[128,224]{1,0:T(8,128)(2,1)S(1)}, u32[]{:S(2)}, u32[]{:S(2)}) collective-permute-start(bf16[128,224]{1,0:T(8,128)(2,1)S(1)} %get-tuple-element.16), channel_id=1, source_target_pairs={{0,64},{1,65},{2,0},{3,1},{4,68},{5,69},{6,4},{7,5},{8,72},{9,73},... | collective-permute-start | bytes 172040 | tf_op jit(solution)/shard_map/ppermute | solution.py:437
  123.6 6.7 %collective-permute-start.4 = (bf16[128,224]{1,0:T(8,128)(2,1)S(1)}, bf16[128,224]{1,0:T(8,128)(2,1)S(1)}, u32[]{:S(2)}, u32[]{:S(2)}) collective-permute-start(bf16[128,224]{1,0:T(8,128)(2,1)S(1)} %get-tuple-element.15), channel_id=1, source_target_pairs={{0,1},{1,0},{2,65},{3,64},{4,5},{5,4},{6,69},{7,68},{8,9},{9,8},{1... | collective-permute-start | bytes 172040 | tf_op jit(solution)/shard_map/ppermute | solution.py:437
  126.0 6.1 %collective-permute-start.3 = (bf16[128,224]{1,0:T(8,128)(2,1)S(1)}, bf16[128,224]{1,0:T(8,128)(2,1)S(1)}, u32[]{:S(2)}, u32[]{:S(2)}) collective-permute-start(bf16[128,224]{1,0:T(8,128)(2,1)S(1)} %get-tuple-element.14), channel_id=1, source_target_pairs={{0,0},{1,1},{2,64},{3,65},{4,4},{5,5},{6,68},{7,69},{8,8},{9,9},{1... | collective-permute-start | bytes 172040 | tf_op jit(solution)/shard_map/ppermute | solution.py:437
